TPU v7x, 256 devices: a whole 4x4x8 slice. The times are simulated.
256 devices in a mesh: gx: 32 (over z, x_hi, core), gy: 8 (over x_lo, y).
Axes of the slice: x: 4 (x_hi: 2, x_lo: 2; x = x_hi * 2 + x_lo), y: 4, z: 8, core: 2. Of those that a mesh axis runs over, the one named last changes fastest.
Arguments:
- head_start: float32 [256, 128, 128], P('gx', 'gy'), may hold values from -6 to 6
- solute_start: float32 [256, 128, 128], P('gx', 'gy'), may hold values from -6 to 6
- source: float32 [256, 128, 128], P('gx', 'gy'), may hold values from -3 to 3
- log_conductivity: float32 [256, 128, 128], P('gx', 'gy'), may hold values from -1 to 1
- dispersivity: float32 [256, 128, 128], P('gx', 'gy'), may hold values from 0.2 to 2
- material: int32 [256, 128, 128], P('gx', 'gy'), may hold values from 0 to 7
- material_table: float32 [8], replicated, may hold values from 0.3 to 3
- boundary: int32 [256, 128], P('gx', 'gy'), may hold values from 0 to 2
- head_weight: float32 [256, 128, 128], P('gx', 'gy'), may hold values from -6 to 6
- solute_weight: float32 [256, 128, 128], P('gx', 'gy'), may hold values from -6 to 6
Outputs:
- head_final: float32 [256, 128, 128], P('gx', 'gy')
- solute_final: float32 [256, 128, 128], P('gx', 'gy')
- grad_conductivity: float32 [256, 128, 128], P('gx', 'gy')
- grad_dispersivity: float32 [256, 128, 128], P('gx', 'gy')
- grad_table: float32 [8], replicated
All inputs are finite; a program needn't handle non-finite values.
Results may differ from a plain program's by a relative error of at most 0.0003.
Values sent between devices are 32-bit elements; how exact they have to be, the bound alone decides.
A program may use at most 128 MiB of HBM per device.

v0:
```python
import jax
import jax.numpy as jnp
from jax import lax
from jax.experimental import pallas as pl
from jax.experimental.pallas import tpu as pltpu
from jax.sharding import PartitionSpec as P

SWEEPS = 8
MATS = 8
coupling_rate = 0.5

BX, BY, NZ, HALO = 8, 16, 128, 8
GX, GY = 32, 8
ROWS = BX + 2 * HALO
COLS = BY + 2 * HALO
PAD = COLS + 16
Y0, Y1 = 8, 8 + COLS
OX, OY = HALO, 8 + HALO
MESH = pl.DeviceIdType.MESH
DIRS = ((1, 0), (-1, 0), (0, 1), (0, -1), (1, 1), (1, -1), (-1, 1), (-1, -1))
HEAD, SOLUTE = 0, 1


def place(lx, ly):
    return (lax.rem(lx + GX, GX), lax.rem(ly + GY, GY))


def x_part(dx):
    return {0: slice(OX, OX + BX), 1: slice(0, HALO), -1: slice(OX + BX, ROWS)}[dx]


def y_from(dy):
    return {0: (0, BY), 1: (BY - HALO, HALO), -1: (0, HALO)}[dy]


def y_into(dy):
    return {0: (HALO, BY), 1: (0, HALO), -1: (HALO + BY, HALO)}[dy]


def up(cells):
    return pltpu.roll(cells, NZ - 1, 1)


def down(cells):
    return pltpu.roll(cells, 1, 1)


def kernel(
    head_in,
    solute_in,
    source_in,
    log_in,
    disp_in,
    material_in,
    table_in,
    boundary_in,
    head_weight_in,
    solute_weight_in,
    head_out,
    solute_out,
    grad_cond_out,
    grad_disp_out,
    grad_table_out,
    first,
    second,
    cx,
    cy,
    czu,
    czd,
    inv,
    rhs,
    xe_head,
    xo_head,
    xe_solute,
    xo_solute,
    lam_even,
    lam_odd,
    acc_side,
    acc_layer,
    acc_drop,
    part_a,
    part_b,
    send_sem,
    recv_sem,
    send_a,
    recv_a,
    send_b,
    recv_b,
):
    gx, gy = lax.axis_index("gx"), lax.axis_index("gy")
    lx, ly = gx, gy
    neighbours = {d: place(lx + d[0], ly + d[1]) for d in DIRS}
    z_at, hi_at, core_at = gx // 4, lax.rem(gx // 2, 2), lax.rem(gx, 2)
    a_at = hi_at * 8 + gy
    b_at = z_at * 2 + core_at

    def a_device(t):
        to = lax.rem(a_at + t, 16)
        return (z_at * 4 + (to // 8) * 2 + core_at, lax.rem(to, 8))

    def b_device(t):
        to = lax.rem(b_at + t, 16)
        return ((to // 2) * 4 + hi_at * 2 + lax.rem(to, 2), gy)

    barrier = pltpu.get_barrier_semaphore()
    for d in DIRS:
        pl.semaphore_signal(barrier, inc=1, device_id=neighbours[d], device_id_type=MESH)
    for t in range(1, 16):
        pl.semaphore_signal(barrier, inc=1, device_id=a_device(t), device_id_type=MESH)
        pl.semaphore_signal(barrier, inc=1, device_id=b_device(t), device_id_type=MESH)

    lane = lax.broadcasted_iota(jnp.int32, (COLS, NZ), 1)
    col = lax.broadcasted_iota(jnp.int32, (COLS, NZ), 0) + (ly * BY - HALO)
    col_in = jnp.where((col >= 0) & (col < GY * BY), 1.0, 0.0)
    col_face = jnp.where((col >= 0) & (col + 1 < GY * BY), 0.5, 0.0)
    top_lane = lane == NZ - 1

    def row_in(i):
        at = lx * BX + (i - HALO)
        return jnp.where((at >= 0) & (at < GX * BX), 1.0, 0.0)

    own = slice(HALO, HALO + BY)
    for r in range(BX):
        material = material_in[r]
        base = jnp.zeros((BY, NZ), jnp.float32)
        for m in range(MATS):
            base = jnp.where(material == m, table_in[m], base)
        conductivity = base * jnp.exp(log_in[r])
        first[1, r, own, :] = conductivity
        first[1, BX + r, own, :] = head_in[r]
        first[1, 2 * BX + r, own, :] = source_in[r]
        second[1, r, own, :] = disp_in[r] * conductivity
        second[1, BX + r, own, :] = solute_in[r]
    kind = boundary_in[...]
    factor = jnp.where(kind == 1, 1.0, jnp.where(kind == 2, 4.0, 0.0)).astype(jnp.float32)
    diagonal_at = lax.broadcasted_iota(jnp.int32, (BY, BY), 0) == lax.broadcasted_iota(
        jnp.int32, (BY, BY), 1
    )
    tops = jnp.zeros((BY, NZ), jnp.float32)
    for r in range(BX):
        spread = jnp.broadcast_to(factor[r : r + 1, :], (BY, BY))
        column = jnp.sum(jnp.where(diagonal_at, spread, 0.0), axis=1, keepdims=True)
        tops = jnp.where(lane[:BY] == r, column, tops)
    first[1, 3 * BX, own, :] = tops

    pl.semaphore_wait(barrier, len(DIRS) + 30)

    def exchange(event, source_of, target_of, dirs=DIRS):
        copies = []
        for d in dirs:
            k = DIRS.index(d)
            copy = pltpu.make_async_remote_copy(
                src_ref=source_of(d),
                dst_ref=target_of(d),
                send_sem=send_sem.at[event, k],
                recv_sem=recv_sem.at[event, k],
                device_id=neighbours[d],
                device_id_type=MESH,
            )
            copy.start()
            copies.append(copy)
        return copies

    def exchange_pack(event, pack):
        def source_of(d):
            start, size = y_from(d[1])
            return pack.at[1, :, pl.ds(HALO + start, size), :]

        def target_of(d):
            start, size = y_into(d[1])
            return pack.at[1 - d[0], :, pl.ds(start, size), :]

        return exchange(event, source_of, target_of)

    def exchange_field(event, ref, *lead, dirs=DIRS):
        def source_of(d):
            start, size = y_from(d[1])
            return ref.at[(*lead, pl.ds(OX, BX), pl.ds(OY + start, size), slice(None))]

        def target_of(d):
            start, size = y_into(d[1])
            part = x_part(d[0])
            return ref.at[
                (*lead, pl.ds(part.start, part.stop - part.start), pl.ds(Y0 + start, size), slice(None))
            ]

        return exchange(event, source_of, target_of, dirs)

    def arrive(copies):
        for copy in copies:
            copy.wait_recv()

    started = []
    got_first = exchange_pack(0, first)
    got_second = exchange_pack(1, second)
    started += got_first + got_second

    own_y = pl.ds(OY, BY)
    wide = pl.ds(Y0, COLS)

    def coefficients(field, value_of):
        row = value_of(0)
        for i in range(ROWS):
            ahead = value_of(i + 1) if i + 1 < ROWS else row
            if i + 1 < ROWS:
                cx[field, i] = (row + ahead) * (0.5 * row_in(i) * row_in(i + 1))
            side = (row + pltpu.roll(row, COLS - 1, 0)) * col_face
            cy[field, i, wide, :] = side
            layer = jnp.where(top_lane, 0.0, 0.5 * (row + up(row)))
            czu[field, i] = layer
            under = down(layer)
            czd[field, i] = under
            if 0 < i < ROWS - 1:
                tile = first[i // BX, 3 * BX, :, :]
                shift = NZ - 1 - i % BX
                top = jnp.where(top_lane, pltpu.roll(tile, shift, 1), 0.0)
                diag = 1.0 + cx[field, i] + cx[field, i - 1] + side + pltpu.roll(side, 1, 0)
                diag = diag + layer + under + top * row
                inv[field, i] = (col_in * row_in(i)) / diag
            row = ahead

    def sweep(field, cur, nxt, lo, hi, right, y_at=0, y_size=COLS):
        here, span = pl.ds(Y0 + y_at, y_size), pl.ds(y_at, y_size)
        ahead, behind = pl.ds(Y0 + y_at + 1, y_size), pl.ds(Y0 + y_at - 1, y_size)
        west, mid = cur[lo - 1, here, :], cur[lo, here, :]
        face_west = cx[field, lo - 1, span, :]
        for i in range(lo, hi):
            east = cur[i + 1, here, :]
            face_east = cx[field, i, span, :]
            total = face_east * east + face_west * west
            total = total + cy[field, i, here, :] * cur[i, ahead, :]
            total = total + cy[field, i, behind, :] * cur[i, behind, :]
            total = total + czu[field, i, span, :] * up(mid) + czd[field, i, span, :] * down(mid)
            if right is not None:
                total = total + right[i, span, :]
            nxt[i, here, :] = total * inv[field, i, span, :]
            west, mid, face_west = mid, east, face_east

    def relax(field, even, odd, base, right):
        def body(t, carry):
            sweep(field, even.at[t], odd.at[t], 1, ROWS - 1, right)
            sweep(field, odd.at[t], even.at[t + 1], 2, ROWS - 2, right)
            return carry

        lax.fori_loop(base, base + 2, body, 0)
        sweep(field, even.at[base + 2], odd.at[base + 2], 5, ROWS - 5, right)
        sweep(field, odd.at[base + 2], even.at[base + 3], 6, ROWS - 6, right)
        sweep(field, even.at[base + 3], odd.at[base + 3], 7, ROWS - 7, right)
        sweep(field, odd.at[base + 3], even.at[base + 4], OX, OX + BX, right, HALO, BY)

    def top_of(r):
        tile = first[1, 3 * BX, own, :]
        return jnp.where(lane[:BY] == NZ - 1, pltpu.roll(tile, NZ - 1 - r, 1), 0.0)

    arrive(got_first)
    coefficients(HEAD, lambda i: first[i // BX, i % BX, :, :])
    for i in range(ROWS):
        start = first[i // BX, BX + i % BX, :, :]
        xe_head[0, i, wide, :] = start
        rhs[i] = start + first[i // BX, 2 * BX + i % BX, :, :]
    relax(HEAD, xe_head, xo_head, 0, rhs)
    got_head1 = exchange_field(2, xe_head, 4)
    started += got_head1

    arrive(got_second)
    coefficients(SOLUTE, lambda i: second[i // BX, i % BX, :, :])
    for i in range(ROWS):
        xe_solute[0, i, wide, :] = second[i // BX, BX + i % BX, :, :]
    for r in range(BX):
        lam_even[0, 0, OX + r, own_y, :] = solute_weight_in[r] * inv[SOLUTE, OX + r, own, :]
    got_lam_s2 = exchange_field(3, lam_even, 0, 0)
    started += got_lam_s2

    arrive(got_head1)
    for i in range(ROWS):
        rhs[i] = xe_head[4, i, wide, :] + first[i // BX, 2 * BX + i % BX, :, :]
    relax(HEAD, xe_head, xo_head, 4, rhs)
    got_head2 = exchange_field(4, xe_head, 8)
    started += got_head2

    for i in range(ROWS):
        rhs[i] = xe_solute[0, i, wide, :] + coupling_rate * xe_head[4, i, wide, :]
    relax(SOLUTE, xe_solute, xo_solute, 0, rhs)
    got_solute1 = exchange_field(5, xe_solute, 4)
    started += got_solute1

    arrive(got_head2)
    arrive(got_solute1)
    for i in range(ROWS):
        rhs[i] = xe_solute[4, i, wide, :] + coupling_rate * xe_head[8, i, wide, :]
    relax(SOLUTE, xe_solute, xo_solute, 4, rhs)
    got_solute2 = exchange_field(6, xe_solute, 8, dirs=DIRS[:4])
    started += got_solute2

    def retrace(field, which):
        relax(field, lam_even.at[which], lam_odd.at[which], 0, None)

    def right_bar(which, r):
        total = lam_even[which, 0, OX + r, own_y, :] + lam_odd[which, 0, OX + r, own_y, :]
        for k in range(1, 4):
            total = total + lam_even[which, k, OX + r, own_y, :]
            total = total + lam_odd[which, k, OX + r, own_y, :]
        return total

    arrive(got_lam_s2)
    retrace(SOLUTE, 0)
    for r in range(BX):
        bar = right_bar(0, r)
        lam_even[1, 0, OX + r, own_y, :] = (head_weight_in[r] + coupling_rate * bar) * inv[
            HEAD, OX + r, own, :
        ]
        lam_even[2, 0, OX + r, own_y, :] = (
            lam_even[0, 4, OX + r, own_y, :] + bar * inv[SOLUTE, OX + r, own, :]
        )
    got_lam_mid = exchange_field(7, lam_even, pl.ds(1, 2), 0)
    started += got_lam_mid

    acc_side[...] = jnp.zeros_like(acc_side)
    acc_layer[...] = jnp.zeros_like(acc_layer)
    acc_drop[...] = jnp.zeros_like(acc_drop)
    north_in = jnp.where(col[own] + 1 < GY * BY, 1.0, 0.0)
    south_in = jnp.where(col[own] > 0, 1.0, 0.0)
    east_in, west_in = row_in(OX + BX), row_in(OX - 1)

    def around(ref, lead, r):
        east, west = ref[(*lead, r + 1, own_y)], ref[(*lead, r - 1, own_y)]
        if r == OX + BX - 1:
            east = east * east_in
        if r == OX:
            west = west * west_in
        north = ref[(*lead, r, pl.ds(OY + 1, BY))] * north_in
        south = ref[(*lead, r, pl.ds(OY - 1, BY))] * south_in
        return east + west + north + south

    def gather(field, even, odd, base, which):
        def body(t, carry):
            steps = (
                ((lam_odd, (which, 3 - t)), (odd, (base + t,)), (even, (base + t,))),
                ((lam_even, (which, 3 - t)), (even, (base + t + 1,)), (odd, (base + t,))),
            )
            for r in range(OX, OX + BX):
                side = acc_side[field, r - OX]
                layer = acc_layer[field, r - OX]
                for (lam, at), _, (old, old_at) in steps:
                    lam_here = lam[(*at, r, own_y)]
                    old_here = old[(*old_at, r, own_y)]
                    side = side + lam_here * around(old, old_at, r)
                    side = side + old_here * around(lam, at, r)
                    layer = layer + lam_here * up(old_here) + old_here * up(lam_here)
                acc_side[field, r - OX] = side
                acc_layer[field, r - OX] = layer
            for r in range(OX - 1, OX + BX + 1):
                drop = acc_drop[field, r - OX + 1, wide, :]
                for (lam, at), (new, new_at), _ in steps:
                    drop = drop + lam[(*at, r, wide)] * new[(*new_at, r, wide)]
                acc_drop[field, r - OX + 1, wide, :] = drop
            return carry

        lax.fori_loop(0, 4, body, 0)

    arrive(got_solute2)
    gather(SOLUTE, xe_solute, xo_solute, 4, 0)
    for r in range(BX):
        head_out[r] = xe_head[8, OX + r, own_y, :]
        solute_out[r] = xe_solute[8, OX + r, own_y, :]

    arrive(got_lam_mid)
    retrace(HEAD, 1)
    retrace(SOLUTE, 2)
    for r in range(BX):
        bar = right_bar(1, r) + coupling_rate * right_bar(2, r)
        lam_even[3, 0, OX + r, own_y, :] = (
            lam_even[1, 4, OX + r, own_y, :] + bar * inv[HEAD, OX + r, own, :]
        )
    got_lam_h1 = exchange_field(8, lam_even, 3, 0)
    started += got_lam_h1
    gather(HEAD, xe_head, xo_head, 4, 1)
    gather(SOLUTE, xe_solute, xo_solute, 0, 2)

    arrive(got_lam_h1)
    retrace(HEAD, 3)
    gather(HEAD, xe_head, xo_head, 0, 3)

    own_lane = lane[:BY]
    inner_top = own_lane < NZ - 1
    inner_low = own_lane > 0

    def sensitivity(field, r):
        layer = jnp.where(inner_top, acc_layer[field, r], 0.0)
        drop = acc_drop[field, r + 1, own_y, :]
        east, west = acc_drop[field, r + 2, own_y, :], acc_drop[field, r, own_y, :]
        count = north_in + south_in
        if r == BX - 1:
            east = east * east_in
        if r == 0:
            west = west * west_in
        count = count + (east_in if r == BX - 1 else 1.0) + (west_in if r == 0 else 1.0)
        count = count + jnp.where(inner_top, 1.0, 0.0) + jnp.where(inner_low, 1.0, 0.0)
        total = acc_side[field, r] + layer + down(layer) - count * drop - east - west
        total = total - acc_drop[field, r + 1, pl.ds(OY + 1, BY), :] * north_in
        total = total - acc_drop[field, r + 1, pl.ds(OY - 1, BY), :] * south_in
        total = total - jnp.where(inner_top, up(drop), 0.0) - jnp.where(inner_low, down(drop), 0.0)
        return 0.5 * total - top_of(r) * drop

    sums = [jnp.zeros((BY, NZ), jnp.float32) for _ in range(MATS)]
    for r in range(BX):
        conductivity = first[1, r, own, :]
        spread_bar = sensitivity(SOLUTE, r)
        total_bar = sensitivity(HEAD, r) + disp_in[r] * spread_bar
        scaled = total_bar * conductivity
        grad_cond_out[r] = scaled
        grad_disp_out[r] = spread_bar * conductivity
        material = material_in[r]
        for m in range(MATS):
            sums[m] = sums[m] + jnp.where(material == m, scaled, 0.0)
    mat_row = lax.broadcasted_iota(jnp.int32, (MATS, NZ), 0)
    partial = jnp.zeros((MATS, NZ), jnp.float32)
    for m in range(MATS):
        partial = jnp.where(mat_row == m, jnp.sum(sums[m], axis=0, keepdims=True), partial)

    def reduce(part, at, device_of, sends, recvs, value):
        part[at] = value
        copies = []
        for t in range(1, 16):
            copies.append(
                pltpu.make_async_remote_copy(
                    src_ref=part.at[at],
                    dst_ref=part.at[at],
                    send_sem=sends.at[t],
                    recv_sem=recvs.at[t],
                    device_id=device_of(t),
                    device_id_type=MESH,
                )
            )
            copies[-1].start()
        for t in range(1, 16):
            slot = lax.rem(at - t + 16, 16)
            pltpu.make_async_remote_copy(
                src_ref=part.at[slot],
                dst_ref=part.at[slot],
                send_sem=sends.at[t],
                recv_sem=recvs.at[t],
                device_id=device_of(t),
                device_id_type=MESH,
            ).wait_recv()
        total = part[0]
        for k in range(1, 16):
            total = total + part[k]
        return copies, total

    copies, partial = reduce(part_a, a_at, a_device, send_a, recv_a, partial)
    started += copies
    copies, partial = reduce(part_b, b_at, b_device, send_b, recv_b, partial)
    started += copies
    base = jnp.ones((MATS, NZ), jnp.float32)
    for m in range(MATS):
        base = jnp.where(mat_row == m, table_in[m], base)
    summed = jnp.sum(partial, axis=1, keepdims=True)
    grad_table_out[...] = jnp.broadcast_to(summed, (MATS, NZ)) / base
    for copy in started:
        copy.wait_send()


def local(*arrays):
    block = jax.ShapeDtypeStruct((BX, BY, NZ), jnp.float32)
    vmem = pl.BlockSpec(memory_space=pltpu.VMEM)
    smem = pl.BlockSpec(memory_space=pltpu.SMEM)
    f32 = jnp.float32
    outs = pl.pallas_call(
        kernel,
        out_shape=(block, block, block, block, jax.ShapeDtypeStruct((MATS, NZ), f32)),
        in_specs=[smem if k == 6 else vmem for k in range(10)],
        out_specs=(vmem,) * 5,
        scratch_shapes=[
            pltpu.VMEM((3, 3 * BX + 1, COLS, NZ), f32),
            pltpu.VMEM((3, 2 * BX, COLS, NZ), f32),
            pltpu.VMEM((2, ROWS, COLS, NZ), f32),
            pltpu.VMEM((2, ROWS, PAD, NZ), f32),
            pltpu.VMEM((2, ROWS, COLS, NZ), f32),
            pltpu.VMEM((2, ROWS, COLS, NZ), f32),
            pltpu.VMEM((2, ROWS, COLS, NZ), f32),
            pltpu.VMEM((ROWS, COLS, NZ), f32),
            pltpu.VMEM((9, ROWS, PAD, NZ), f32),
            pltpu.VMEM((8, ROWS, PAD, NZ), f32),
            pltpu.VMEM((9, ROWS, PAD, NZ), f32),
            pltpu.VMEM((8, ROWS, PAD, NZ), f32),
            pltpu.VMEM((4, 5, ROWS, PAD, NZ), f32),
            pltpu.VMEM((4, 4, ROWS, PAD, NZ), f32),
            pltpu.VMEM((2, BX, BY, NZ), f32),
            pltpu.VMEM((2, BX, BY, NZ), f32),
            pltpu.VMEM((2, BX + 2, PAD, NZ), f32),
            pltpu.VMEM((16, MATS, NZ), f32),
            pltpu.VMEM((16, MATS, NZ), f32),
            pltpu.SemaphoreType.DMA((9, 8)),
            pltpu.SemaphoreType.DMA((9, 8)),
            pltpu.SemaphoreType.DMA((16,)),
            pltpu.SemaphoreType.DMA((16,)),
            pltpu.SemaphoreType.DMA((16,)),
            pltpu.SemaphoreType.DMA((16,)),
        ],
        compiler_params=pltpu.CompilerParams(
            collective_id=0, has_side_effects=True, vmem_limit_bytes=58 << 20
        ),
        name="window",
    )(*arrays)
    return (*outs[:4], outs[4][:, 0])


def solution(mesh):
    block = P("gx", "gy", None)
    return jax.shard_map(
        local,
        mesh=mesh,
        in_specs=(block, block, block, block, block, block, P(), P("gx", "gy"), block, block),
        out_specs=(block, block, block, block, P()),
        check_vma=False,
    )
```

profile of v0, /device:TPU:1, one launch (start us, length us, event | category | flops | bytes accessed | tf_op | source)
XLA Modules:
  0.0 92.0 jit_solution(7201549716081543650)
XLA Ops:
  0.6 86.2 %window.1 = (f32[8,16,128]{2,1,0:T(8,128)}, f32[8,16,128]{2,1,0:T(8,128)}, f32[8,16,128]{2,1,0:T(8,128)}, f32[8,16,128]{2,1,0:T(8,128)}, f32[8,128]{1,0:T(8,128)}) custom-call(f32[8,16,128]{2,1,0:T(8,128)} %head_in.1, f32[8,16,128]{2,1,0:T(8,128)} %solute_in.1, f32[8,16,128]{2,1,0:T(8,128)} %source_in.1, f32[8,16,128]{2,1,0:T(8,128)} %log_in.1, ...), custom_call_target="tpu_custom_call" | custom-call | tf_op jit(solution)/shard_map/window/pallas_call | solution.py:469
  86.8 0.0 copy-start.3
  86.8 0.7 copy-done.3
  87.5 0.6 slice_reduce_fusion
  88.1 0.0 copy-start.2
  88.1 1.5 %copy.19 = f32[8,16,128]{2,1,0:T(8,128)} copy(f32[8,16,128]{2,1,0:T(8,128)} %get-tuple-element.20) | data formatting | bytes 131072
  89.6 0.0 copy-done.2
  89.6 0.0 copy-start.1
  89.6 0.6 copy.20
  90.3 0.2 copy-done.1
  90.5 0.0 copy-start
  90.5 0.6 copy.21
  91.1 0.2 copy-done
  91.4 0.6 copy.22
Async XLA Ops:
  86.8 0.7 copy-start.3
  88.1 1.5 %copy-start.2 = (f32[8,16,128]{2,1,0:T(8,128)S(1)}, f32[8,16,128]{2,1,0:T(8,128)}, u32[]{:S(2)}) copy-start(f32[8,16,128]{2,1,0:T(8,128)} %get-tuple-element.21) | copy-start | bytes 196612
  89.6 0.9 copy-start.1
  90.5 0.9 copy-start
where the time goes:
time: 92.3 us; the launch traced here: 92 us
  Pallas kernels  86.2 us (93%)
  local copies, waits for them, and re-layouts  5.16 us (6%)
    pallas_call x1, Pallas kernels, local(): pl.pallas_call(kernel, out_shape=(block, block, block, block, jax.ShapeDt...  86.2 us
    unnamed x12, local copies, waits for them, and re-layouts  4.53 us

commit v1 on v0

--- a/solution.py
+++ b/solution.py
@@ -18,6 +18,9 @@
 OX, OY = HALO, 8 + HALO
 MESH = pl.DeviceIdType.MESH
 DIRS = ((1, 0), (-1, 0), (0, 1), (0, -1), (1, 1), (1, -1), (-1, 1), (-1, -1))
+FAR = ((2, 0), (-2, 0))
+FACES, CORNERS = DIRS[:4], DIRS[4:]
+TILES = 50
 HEAD, SOLUTE = 0, 1
 
 
@@ -35,6 +38,12 @@
 
 def y_into(dy):
     return {0: (HALO, BY), 1: (0, HALO), -1: (HALO + BY, HALO)}[dy]
+
+
+CORNER_ROWS = {
+    8: ((1, 7, 7), (2, 6, 6), (3, 5, 5), (4, None, 4)),
+    9: ((1, None, 8), (2, 8, 7), (3, 7, 6), (4, 6, 5), (5, None, 4)),
+}
 
 
 def up(cells):
@@ -56,13 +65,14 @@
     boundary_in,
     head_weight_in,
     solute_weight_in,
-    head_out,
-    solute_out,
-    grad_cond_out,
-    grad_disp_out,
+    fields_out,
     grad_table_out,
     first,
     second,
+    far_x,
+    far_y,
+    corner_out,
+    corner_in,
     cx,
     cy,
     czu,
@@ -82,6 +92,8 @@
     part_b,
     send_sem,
     recv_sem,
+    send_far,
+    recv_far,
     send_a,
     recv_a,
     send_b,
@@ -89,7 +101,7 @@
 ):
     gx, gy = lax.axis_index("gx"), lax.axis_index("gy")
     lx, ly = gx, gy
-    neighbours = {d: place(lx + d[0], ly + d[1]) for d in DIRS}
+    neighbours = {d: place(lx + d[0], ly + d[1]) for d in (*DIRS, *FAR)}
     z_at, hi_at, core_at = gx // 4, lax.rem(gx // 2, 2), lax.rem(gx, 2)
     a_at = hi_at * 8 + gy
     b_at = z_at * 2 + core_at
@@ -103,7 +115,7 @@
         return ((to // 2) * 4 + hi_at * 2 + lax.rem(to, 2), gy)
 
     barrier = pltpu.get_barrier_semaphore()
-    for d in DIRS:
+    for d in (*DIRS, *FAR):
         pl.semaphore_signal(barrier, inc=1, device_id=neighbours[d], device_id_type=MESH)
     for t in range(1, 16):
         pl.semaphore_signal(barrier, inc=1, device_id=a_device(t), device_id_type=MESH)
@@ -120,6 +132,8 @@
         return jnp.where((at >= 0) & (at < GX * BX), 1.0, 0.0)
 
     own = slice(HALO, HALO + BY)
+    own_y = pl.ds(OY, BY)
+    wide = pl.ds(Y0, COLS)
     for r in range(BX):
         material = material_in[r]
         base = jnp.zeros((BY, NZ), jnp.float32)
@@ -130,7 +144,8 @@
         first[1, BX + r, own, :] = head_in[r]
         first[1, 2 * BX + r, own, :] = source_in[r]
         second[1, r, own, :] = disp_in[r] * conductivity
-        second[1, BX + r, own, :] = solute_in[r]
+        second[1, BX + r, own, :] = solute_weight_in[r]
+        xe_solute[0, OX + r, own_y, :] = solute_in[r]
     kind = boundary_in[...]
     factor = jnp.where(kind == 1, 1.0, jnp.where(kind == 2, 4.0, 0.0)).astype(jnp.float32)
     diagonal_at = lax.broadcasted_iota(jnp.int32, (BY, BY), 0) == lax.broadcasted_iota(
@@ -143,81 +158,191 @@
         tops = jnp.where(lane[:BY] == r, column, tops)
     first[1, 3 * BX, own, :] = tops
 
-    pl.semaphore_wait(barrier, len(DIRS) + 30)
-
-    def exchange(event, source_of, target_of, dirs=DIRS):
-        copies = []
-        for d in dirs:
-            k = DIRS.index(d)
-            copy = pltpu.make_async_remote_copy(
-                src_ref=source_of(d),
-                dst_ref=target_of(d),
-                send_sem=send_sem.at[event, k],
-                recv_sem=recv_sem.at[event, k],
-                device_id=neighbours[d],
-                device_id_type=MESH,
+    pl.semaphore_wait(barrier, len(DIRS) + len(FAR) + 30)
+
+    near = lax.broadcasted_iota(jnp.int32, (HALO, NZ), 0)
+
+    def launch(event, d, source, target):
+        k = DIRS.index(d)
+        copy = pltpu.make_async_remote_copy(
+            src_ref=source,
+            dst_ref=target,
+            send_sem=send_sem.at[event, k],
+            recv_sem=recv_sem.at[event, k],
+            device_id=neighbours[d],
+            device_id_type=MESH,
+        )
+        copy.start()
+        return copy
+
+    def exchange(event, source_of, target_of, base, fields, extra=None):
+        copies = [launch(event, d, source_of(d), target_of(d)) for d in FACES]
+        for k, (dx, dy) in enumerate(CORNERS):
+            at = base
+            for radius, read, _ in fields:
+                for d, partner, cells in CORNER_ROWS[radius]:
+                    tile = read(d, dx, dy)
+                    if partner is not None:
+                        other = read(partner, dx, dy)
+                        if dy > 0:
+                            tile = jnp.where(near >= HALO - cells, tile, pltpu.roll(other, HALO - cells, 0))
+                        else:
+                            tile = jnp.where(near < cells, tile, pltpu.roll(other, cells, 0))
+                    corner_out[k, at] = tile
+                    at += 1
+            if extra is not None:
+                corner_out[k, at] = extra[0](dx, dy)
+                at += 1
+            part = pl.ds(base, at - base)
+            copies.append(launch(event, (dx, dy), corner_out.at[k, part], corner_in.at[k, part]))
+
+        def lay():
+            for k, (dx, dy) in enumerate(CORNERS):
+                at = base
+                for radius, _, write in fields:
+                    for d, partner, cells in CORNER_ROWS[radius]:
+                        tile = corner_in[k, at]
+                        write(d, dx, dy, tile)
+                        if partner is not None:
+                            back = cells if dy > 0 else HALO - cells
+                            write(partner, dx, dy, pltpu.roll(tile, back, 0))
+                        at += 1
+                if extra is not None:
+                    extra[1](dx, dy, corner_in[k, at])
+
+        started.extend(copies)
+        return copies, lay
+
+    def exchange_pack(event, pack, base, radii, extra=None):
+        def source_of(d):
+            first_col, size = y_from(d[1])
+            return pack.at[1, :, pl.ds(HALO + first_col, size), :]
+
+        def target_of(d):
+            first_col, size = y_into(d[1])
+            return pack.at[1 - d[0], :, pl.ds(first_col, size), :]
+
+        def field(f, radius):
+            def row(d, dx):
+                return f * BX + (BX - d if dx > 0 else d - 1)
+
+            def read(d, dx, dy):
+                return pack[1, row(d, dx), pl.ds(HALO + y_from(dy)[0], HALO), :]
+
+            def write(d, dx, dy, tile):
+                pack[1 - dx, row(d, dx), pl.ds(y_into(dy)[0], HALO), :] = tile
+
+            return radius, read, write
+
+        fields = [field(f, radius) for f, radius in enumerate(radii)]
+        if extra is not None:
+            at = extra
+            extra = (
+                lambda dx, dy: pack[1, at, pl.ds(HALO + y_from(dy)[0], HALO), :],
+                lambda dx, dy, tile: pack.__setitem__(
+                    (1 - dx, at, pl.ds(y_into(dy)[0], HALO), slice(None)), tile
+                ),
             )
-            copy.start()
-            copies.append(copy)
-        return copies
-
-    def exchange_pack(event, pack):
+        return exchange(event, source_of, target_of, base, fields, extra)
+
+    def exchange_field(event, ref, base, *leads, faces=None):
+        lead_all = faces or leads[0]
+
         def source_of(d):
-            start, size = y_from(d[1])
-            return pack.at[1, :, pl.ds(HALO + start, size), :]
+            first_col, size = y_from(d[1])
+            return ref.at[(*lead_all, pl.ds(OX, BX), pl.ds(OY + first_col, size), slice(None))]
 
         def target_of(d):
-            start, size = y_into(d[1])
-            return pack.at[1 - d[0], :, pl.ds(start, size), :]
-
-        return exchange(event, source_of, target_of)
-
-    def exchange_field(event, ref, *lead, dirs=DIRS):
-        def source_of(d):
-            start, size = y_from(d[1])
-            return ref.at[(*lead, pl.ds(OX, BX), pl.ds(OY + start, size), slice(None))]
-
-        def target_of(d):
-            start, size = y_into(d[1])
+            first_col, size = y_into(d[1])
             part = x_part(d[0])
-            return ref.at[
-                (*lead, pl.ds(part.start, part.stop - part.start), pl.ds(Y0 + start, size), slice(None))
-            ]
-
-        return exchange(event, source_of, target_of, dirs)
-
-    def arrive(copies):
+            rows = pl.ds(part.start, part.stop - part.start)
+            return ref.at[(*lead_all, rows, pl.ds(Y0 + first_col, size), slice(None))]
+
+        def field(lead):
+            def read(d, dx, dy):
+                row = OX + BX - d if dx > 0 else OX + d - 1
+                return ref[(*lead, row, pl.ds(OY + y_from(dy)[0], HALO))]
+
+            def write(d, dx, dy, tile):
+                row = OX - d if dx > 0 else OX + BX - 1 + d
+                ref[(*lead, row, pl.ds(Y0 + y_into(dy)[0], HALO))] = tile
+
+            return HALO, read, write
+
+        if base is None:
+            copies = [launch(event, d, source_of(d), target_of(d)) for d in FACES]
+            started.extend(copies)
+            return copies, None
+        return exchange(event, source_of, target_of, base, [field(lead) for lead in leads])
+
+    def arrive(got):
+        copies, lay = got
         for copy in copies:
             copy.wait_recv()
+        if lay is not None:
+            lay()
+
+    def send_to(d, source, target, k):
+        copy = pltpu.make_async_remote_copy(
+            src_ref=source,
+            dst_ref=target,
+            send_sem=send_far.at[k],
+            recv_sem=recv_far.at[k],
+            device_id=neighbours[d],
+            device_id_type=MESH,
+        )
+        copy.start()
+        return copy
 
     started = []
-    got_first = exchange_pack(0, first)
-    got_second = exchange_pack(1, second)
-    started += got_first + got_second
-
-    own_y = pl.ds(OY, BY)
-    wide = pl.ds(Y0, COLS)
-
-    def coefficients(field, value_of):
+    got_first = exchange_pack(0, first, 0, (8, 8, 8), 3 * BX)
+    got_second = exchange_pack(1, second, 13, (9, 8))
+    rows = pl.ds(0, BX)
+    got_far = [
+        send_to((2, 0), second.at[1, BX - 1, pl.ds(HALO, BY), :], far_x.at[0], 0),
+        send_to((-2, 0), second.at[1, 0, pl.ds(HALO, BY), :], far_x.at[1], 1),
+        send_to((0, 1), second.at[1, rows, pl.ds(HALO, HALO), :], far_y.at[0], 2),
+        send_to((0, -1), second.at[1, rows, pl.ds(BY, HALO), :], far_y.at[1], 3),
+    ]
+    started += got_far
+    got_start = exchange_field(2, xe_solute, 22, (0,))
+
+    at_low, at_high = col == ly * BY - HALO, col == ly * BY + BY + HALO - 1
+    low_face = jnp.where(at_low & (col > 0) & (col < GY * BY), 0.5, 0.0)
+
+    def coefficients(field, value_of, beyond):
         row = value_of(0)
+        face_before = None
+        if beyond:
+            face_before = (value_of(-1) + row) * (0.5 * row_in(-1) * row_in(0))
         for i in range(ROWS):
-            ahead = value_of(i + 1) if i + 1 < ROWS else row
-            if i + 1 < ROWS:
-                cx[field, i] = (row + ahead) * (0.5 * row_in(i) * row_in(i + 1))
-            side = (row + pltpu.roll(row, COLS - 1, 0)) * col_face
+            face = None
+            if beyond or i + 1 < ROWS:
+                ahead = value_of(i + 1)
+                face = (row + ahead) * (0.5 * row_in(i) * row_in(i + 1))
+                if i + 1 < ROWS:
+                    cx[field, i] = face
+            north = pltpu.roll(row, COLS - 1, 0)
+            far = beyond and OX <= i < OX + BX
+            if far:
+                north = jnp.where(at_high, far_y[1, i - OX, 0:1, :], north)
+            side = (row + north) * col_face
             cy[field, i, wide, :] = side
             layer = jnp.where(top_lane, 0.0, 0.5 * (row + up(row)))
             czu[field, i] = layer
             under = down(layer)
             czd[field, i] = under
-            if 0 < i < ROWS - 1:
+            if face is not None and face_before is not None:
+                south = pltpu.roll(side, 1, 0)
+                if far:
+                    low = (row + far_y[0, i - OX, HALO - 1 : HALO, :]) * low_face
+                    south = jnp.where(at_low, low, south)
                 tile = first[i // BX, 3 * BX, :, :]
-                shift = NZ - 1 - i % BX
-                top = jnp.where(top_lane, pltpu.roll(tile, shift, 1), 0.0)
-                diag = 1.0 + cx[field, i] + cx[field, i - 1] + side + pltpu.roll(side, 1, 0)
-                diag = diag + layer + under + top * row
+                top = jnp.where(top_lane, pltpu.roll(tile, NZ - 1 - i % BX, 1), 0.0)
+                diag = 1.0 + face + face_before + side + south + layer + under + top * row
                 inv[field, i] = (col_in * row_in(i)) / diag
-            row = ahead
+            if face is not None:
+                row, face_before = ahead, face
 
     def sweep(field, cur, nxt, lo, hi, right, y_at=0, y_size=COLS):
         here, span = pl.ds(Y0 + y_at, y_size), pl.ds(y_at, y_size)
@@ -252,46 +377,6 @@
         tile = first[1, 3 * BX, own, :]
         return jnp.where(lane[:BY] == NZ - 1, pltpu.roll(tile, NZ - 1 - r, 1), 0.0)
 
-    arrive(got_first)
-    coefficients(HEAD, lambda i: first[i // BX, i % BX, :, :])
-    for i in range(ROWS):
-        start = first[i // BX, BX + i % BX, :, :]
-        xe_head[0, i, wide, :] = start
-        rhs[i] = start + first[i // BX, 2 * BX + i % BX, :, :]
-    relax(HEAD, xe_head, xo_head, 0, rhs)
-    got_head1 = exchange_field(2, xe_head, 4)
-    started += got_head1
-
-    arrive(got_second)
-    coefficients(SOLUTE, lambda i: second[i // BX, i % BX, :, :])
-    for i in range(ROWS):
-        xe_solute[0, i, wide, :] = second[i // BX, BX + i % BX, :, :]
-    for r in range(BX):
-        lam_even[0, 0, OX + r, own_y, :] = solute_weight_in[r] * inv[SOLUTE, OX + r, own, :]
-    got_lam_s2 = exchange_field(3, lam_even, 0, 0)
-    started += got_lam_s2
-
-    arrive(got_head1)
-    for i in range(ROWS):
-        rhs[i] = xe_head[4, i, wide, :] + first[i // BX, 2 * BX + i % BX, :, :]
-    relax(HEAD, xe_head, xo_head, 4, rhs)
-    got_head2 = exchange_field(4, xe_head, 8)
-    started += got_head2
-
-    for i in range(ROWS):
-        rhs[i] = xe_solute[0, i, wide, :] + coupling_rate * xe_head[4, i, wide, :]
-    relax(SOLUTE, xe_solute, xo_solute, 0, rhs)
-    got_solute1 = exchange_field(5, xe_solute, 4)
-    started += got_solute1
-
-    arrive(got_head2)
-    arrive(got_solute1)
-    for i in range(ROWS):
-        rhs[i] = xe_solute[4, i, wide, :] + coupling_rate * xe_head[8, i, wide, :]
-    relax(SOLUTE, xe_solute, xo_solute, 4, rhs)
-    got_solute2 = exchange_field(6, xe_solute, 8, dirs=DIRS[:4])
-    started += got_solute2
-
     def retrace(field, which):
         relax(field, lam_even.at[which], lam_odd.at[which], 0, None)
 
@@ -301,19 +386,6 @@
             total = total + lam_even[which, k, OX + r, own_y, :]
             total = total + lam_odd[which, k, OX + r, own_y, :]
         return total
-
-    arrive(got_lam_s2)
-    retrace(SOLUTE, 0)
-    for r in range(BX):
-        bar = right_bar(0, r)
-        lam_even[1, 0, OX + r, own_y, :] = (head_weight_in[r] + coupling_rate * bar) * inv[
-            HEAD, OX + r, own, :
-        ]
-        lam_even[2, 0, OX + r, own_y, :] = (
-            lam_even[0, 4, OX + r, own_y, :] + bar * inv[SOLUTE, OX + r, own, :]
-        )
-    got_lam_mid = exchange_field(7, lam_even, pl.ds(1, 2), 0)
-    started += got_lam_mid
 
     acc_side[...] = jnp.zeros_like(acc_side)
     acc_layer[...] = jnp.zeros_like(acc_layer)
@@ -358,12 +430,48 @@
 
         lax.fori_loop(0, 4, body, 0)
 
-    arrive(got_solute2)
-    gather(SOLUTE, xe_solute, xo_solute, 4, 0)
+    arrive(got_first)
+    coefficients(HEAD, lambda i: first[i // BX, i % BX, :, :], False)
+    for i in range(ROWS):
+        start = first[i // BX, BX + i % BX, :, :]
+        xe_head[0, i, wide, :] = start
+        rhs[i] = start + first[i // BX, 2 * BX + i % BX, :, :]
+    relax(HEAD, xe_head, xo_head, 0, rhs)
+    got_head1 = exchange_field(3, xe_head, 26, (4,))
+
+    arrive(got_second)
+    arrive((got_far, None))
+
+    def spreading(i):
+        if 0 <= i < ROWS:
+            return second[i // BX, i % BX, :, :]
+        beyond = far_x[0 if i < 0 else 1]
+        return jnp.concatenate([beyond[:HALO], beyond, beyond[:HALO]], axis=0)
+
+    coefficients(SOLUTE, spreading, True)
+    for i in range(ROWS):
+        lam_even[0, 0, i, wide, :] = second[i // BX, BX + i % BX, :, :] * inv[SOLUTE, i]
+    retrace(SOLUTE, 0)
     for r in range(BX):
-        head_out[r] = xe_head[8, OX + r, own_y, :]
-        solute_out[r] = xe_solute[8, OX + r, own_y, :]
-
+        bar = right_bar(0, r)
+        lam_even[1, 0, OX + r, own_y, :] = (head_weight_in[r] + coupling_rate * bar) * inv[
+            HEAD, OX + r, own, :
+        ]
+        lam_even[2, 0, OX + r, own_y, :] = (
+            lam_even[0, 4, OX + r, own_y, :] + bar * inv[SOLUTE, OX + r, own, :]
+        )
+    got_lam_mid = exchange_field(4, lam_even, 30, (1, 0), (2, 0), faces=(pl.ds(1, 2), 0))
+
+    arrive(got_head1)
+    for i in range(ROWS):
+        rhs[i] = xe_head[4, i, wide, :] + first[i // BX, 2 * BX + i % BX, :, :]
+    relax(HEAD, xe_head, xo_head, 4, rhs)
+    got_head2 = exchange_field(5, xe_head, 38, (8,))
+    arrive(got_start)
+    for i in range(ROWS):
+        rhs[i] = xe_solute[0, i, wide, :] + coupling_rate * xe_head[4, i, wide, :]
+    relax(SOLUTE, xe_solute, xo_solute, 0, rhs)
+    got_solute1 = exchange_field(6, xe_solute, 42, (4,))
     arrive(got_lam_mid)
     retrace(HEAD, 1)
     retrace(SOLUTE, 2)
@@ -372,14 +480,24 @@
         lam_even[3, 0, OX + r, own_y, :] = (
             lam_even[1, 4, OX + r, own_y, :] + bar * inv[HEAD, OX + r, own, :]
         )
-    got_lam_h1 = exchange_field(8, lam_even, 3, 0)
-    started += got_lam_h1
+    got_lam_h1 = exchange_field(7, lam_even, 46, (3, 0))
+
+    arrive(got_head2)
+    arrive(got_solute1)
+    for i in range(ROWS):
+        rhs[i] = xe_solute[4, i, wide, :] + coupling_rate * xe_head[8, i, wide, :]
+    relax(SOLUTE, xe_solute, xo_solute, 4, rhs)
+    got_solute2 = exchange_field(8, xe_solute, None, (8,))
     gather(HEAD, xe_head, xo_head, 4, 1)
     gather(SOLUTE, xe_solute, xo_solute, 0, 2)
-
     arrive(got_lam_h1)
     retrace(HEAD, 3)
     gather(HEAD, xe_head, xo_head, 0, 3)
+    for r in range(BX):
+        fields_out[0, r] = xe_head[8, OX + r, own_y, :]
+        fields_out[1, r] = xe_solute[8, OX + r, own_y, :]
+    arrive(got_solute2)
+    gather(SOLUTE, xe_solute, xo_solute, 4, 0)
 
     own_lane = lane[:BY]
     inner_top = own_lane < NZ - 1
@@ -408,8 +526,8 @@
         spread_bar = sensitivity(SOLUTE, r)
         total_bar = sensitivity(HEAD, r) + disp_in[r] * spread_bar
         scaled = total_bar * conductivity
-        grad_cond_out[r] = scaled
-        grad_disp_out[r] = spread_bar * conductivity
+        fields_out[2, r] = scaled
+        fields_out[3, r] = spread_bar * conductivity
         material = material_in[r]
         for m in range(MATS):
             sums[m] = sums[m] + jnp.where(material == m, scaled, 0.0)
@@ -461,19 +579,33 @@
         copy.wait_send()
 
 
+def hand_over(fields, table, head_out, solute_out, grad_cond_out, grad_disp_out, grad_table_out):
+    for k, out in enumerate((head_out, solute_out, grad_cond_out, grad_disp_out)):
+        out[...] = fields[k]
+    for m in range(MATS):
+        grad_table_out[m] = table[m, 0]
+
+
 def local(*arrays):
-    block = jax.ShapeDtypeStruct((BX, BY, NZ), jnp.float32)
+    f32 = jnp.float32
+    block = jax.ShapeDtypeStruct((BX, BY, NZ), f32)
     vmem = pl.BlockSpec(memory_space=pltpu.VMEM)
     smem = pl.BlockSpec(memory_space=pltpu.SMEM)
-    f32 = jnp.float32
-    outs = pl.pallas_call(
+    fields, table = pl.pallas_call(
         kernel,
-        out_shape=(block, block, block, block, jax.ShapeDtypeStruct((MATS, NZ), f32)),
+        out_shape=(
+            jax.ShapeDtypeStruct((4, BX, BY, NZ), f32),
+            jax.ShapeDtypeStruct((MATS, NZ), f32),
+        ),
         in_specs=[smem if k == 6 else vmem for k in range(10)],
-        out_specs=(vmem,) * 5,
+        out_specs=(vmem, vmem),
         scratch_shapes=[
             pltpu.VMEM((3, 3 * BX + 1, COLS, NZ), f32),
             pltpu.VMEM((3, 2 * BX, COLS, NZ), f32),
+            pltpu.VMEM((2, BY, NZ), f32),
+            pltpu.VMEM((2, BX, HALO, NZ), f32),
+            pltpu.VMEM((4, TILES, HALO, NZ), f32),
+            pltpu.VMEM((4, TILES, HALO, NZ), f32),
             pltpu.VMEM((2, ROWS, COLS, NZ), f32),
             pltpu.VMEM((2, ROWS, PAD, NZ), f32),
             pltpu.VMEM((2, ROWS, COLS, NZ), f32),
@@ -493,6 +625,8 @@
             pltpu.VMEM((16, MATS, NZ), f32),
             pltpu.SemaphoreType.DMA((9, 8)),
             pltpu.SemaphoreType.DMA((9, 8)),
+            pltpu.SemaphoreType.DMA((4,)),
+            pltpu.SemaphoreType.DMA((4,)),
             pltpu.SemaphoreType.DMA((16,)),
             pltpu.SemaphoreType.DMA((16,)),
             pltpu.SemaphoreType.DMA((16,)),
@@ -503,7 +637,13 @@
         ),
         name="window",
     )(*arrays)
-    return (*outs[:4], outs[4][:, 0])
+    return pl.pallas_call(
+        hand_over,
+        out_shape=(block, block, block, block, jax.ShapeDtypeStruct((MATS,), f32)),
+        in_specs=[vmem, vmem],
+        out_specs=(vmem,) * 4 + (smem,),
+        name="hand_over",
+    )(fields, table)
 
 
 def solution(mesh):

time: 92.3 us -> 71.5 us (0.77)
  Pallas kernels: 86.2 us -> 70.7 us
  local copies, waits for them, and re-layouts: 5.16 us -> 0 us
    pallas_call x1 -> x2, Pallas kernels: 86.2 us -> 70.7 us  [the longest x1 69 us: local(): pl.pallas_call(kernel, out_shape=(jax.ShapeDtypeStruct((4, BX, BY, NZ), f...]
    unnamed x12 -> x0, local copies, waits for them, and re-layouts: 4.53 us -> none
where the time goes in v1:
time: 71.5 us; the launch traced here: 71.3 us
  Pallas kernels  70.7 us (99%)
    pallas_call x1, Pallas kernels, local(): pl.pallas_call(kernel, out_shape=(jax.ShapeDtypeStruct((4, BX, BY, NZ), f...  69 us
    pallas_call x1, Pallas kernels, local(): pl.pallas_call(hand_over, out_shape=(block, block, block, block, jax.Shap...  1.67 us

profile of v1, /device:TPU:1, one launch (start us, length us, event | category | flops | bytes accessed | tf_op | source)
XLA Modules:
  0.0 71.3 jit_solution(372380416851626985)
XLA Ops:
  0.6 69.0 %window.1 = (f32[4,8,16,128]{3,2,1,0:T(8,128)}, f32[8,128]{1,0:T(8,128)}) custom-call(f32[8,16,128]{2,1,0:T(8,128)} %head_in.1, f32[8,16,128]{2,1,0:T(8,128)} %solute_in.1, f32[8,16,128]{2,1,0:T(8,128)} %source_in.1, f32[8,16,128]{2,1,0:T(8,128)} %log_in.1, f32[8,16,128]{2,1,0:T(8,128)} %disp_in.1, s32[8,16,128]{2,1,0:T(8,128)} %material_in.1, f32[8]{0:T(128)} %table_in.1, ...), custom_call_target="tpu_custom_call" | custom-call | tf_op jit(solution)/shard_map/window/pallas_call | solution.py:594
  69.6 1.7 %hand_over.1 = (f32[8,16,128]{2,1,0:T(8,128)}, f32[8,16,128]{2,1,0:T(8,128)}, f32[8,16,128]{2,1,0:T(8,128)}, f32[8,16,128]{2,1,0:T(8,128)}, f32[8]{0:T(128)}) custom-call(f32[4,8,16,128]{3,2,1,0:T(8,128)} %get-tuple-element.7.fields, f32[8,128]{1,0:T(8,128)} %get-tuple-element.8.table), custom_call_target="tpu_custom_call" | custom-call | tf_op jit(solution)/shard_map/hand_over/pallas_call | solution.py:640

commit v2 on v1

--- a/solution.py
+++ b/solution.py
@@ -24,8 +24,24 @@
 HEAD, SOLUTE = 0, 1
 
 
-def place(lx, ly):
-    return (lax.rem(lx + GX, GX), lax.rem(ly + GY, GY))
+def host_of(bx, by):
+    z, half = bx // 4, by // 4
+    pair = lax.rem(lax.rem(bx // 2, 2) + z, 2)
+    x = jnp.where(half == 0, pair, 3 - pair)
+    y = jnp.where(half == 0, lax.rem(by, 4), 3 - lax.rem(by, 4))
+    return (z * 4 + (x // 2) * 2 + lax.rem(bx, 2), lax.rem(x, 2) * 4 + y)
+
+
+def block_of(gx, gy):
+    z, x, y = gx // 4, lax.rem(gx // 2, 2) * 2 + gy // 4, lax.rem(gy, 4)
+    half = x // 2
+    pair = jnp.where(half == 0, x, 3 - x)
+    high = lax.rem(pair + z, 2)
+    return (z * 4 + high * 2 + lax.rem(gx, 2), half * 4 + jnp.where(half == 0, y, 3 - y))
+
+
+def place(bx, by):
+    return host_of(lax.rem(bx + GX, GX), lax.rem(by + GY, GY))
 
 
 def x_part(dx):
@@ -55,18 +71,32 @@
 
 
 def kernel(
-    head_in,
-    solute_in,
-    source_in,
+    head_hbm,
+    solute_hbm,
+    source_hbm,
+    log_hbm,
+    disp_hbm,
+    material_hbm,
+    table_in,
+    boundary_hbm,
+    head_weight_hbm,
+    solute_weight_hbm,
+    fields_out,
+    grad_table_out,
     log_in,
-    disp_in,
     material_in,
-    table_in,
     boundary_in,
     head_weight_in,
-    solute_weight_in,
-    fields_out,
-    grad_table_out,
+    grads,
+    material_home,
+    disp_home,
+    made,
+    tops_home,
+    load_sem,
+    store_sem,
+    store_send,
+    move_send,
+    move_recv,
     first,
     second,
     far_x,
@@ -76,7 +106,6 @@
     cx,
     cy,
     czu,
-    czd,
     inv,
     rhs,
     xe_head,
@@ -100,7 +129,10 @@
     recv_b,
 ):
     gx, gy = lax.axis_index("gx"), lax.axis_index("gy")
-    lx, ly = gx, gy
+    lx, ly = block_of(gx, gy)
+    host, home = host_of(gx, gy), (lx, ly)
+    stays = (lx == gx) & (ly == gy)
+    moves = jnp.logical_not(stays)
     neighbours = {d: place(lx + d[0], ly + d[1]) for d in (*DIRS, *FAR)}
     z_at, hi_at, core_at = gx // 4, lax.rem(gx // 2, 2), lax.rem(gx, 2)
     a_at = hi_at * 8 + gy
@@ -113,6 +145,23 @@
     def b_device(t):
         to = lax.rem(b_at + t, 16)
         return ((to // 2) * 4 + hi_at * 2 + lax.rem(to, 2), gy)
+
+    own = slice(HALO, HALO + BY)
+    own_y = pl.ds(OY, BY)
+    wide = pl.ds(Y0, COLS)
+
+    def center(pack, f):
+        return pack.at[1, pl.ds(f * BX, BX), pl.ds(HALO, BY), :]
+
+    loads = []
+    for source, target in (
+        (boundary_hbm, boundary_in),
+        (log_hbm, log_in),
+        (material_hbm, material_home),
+        (disp_hbm, disp_home),
+    ):
+        loads.append(pltpu.make_async_copy(source, target, load_sem.at[len(loads)]))
+        loads[-1].start()
 
     barrier = pltpu.get_barrier_semaphore()
     for d in (*DIRS, *FAR):
@@ -121,6 +170,11 @@
         pl.semaphore_signal(barrier, inc=1, device_id=a_device(t), device_id_type=MESH)
         pl.semaphore_signal(barrier, inc=1, device_id=b_device(t), device_id_type=MESH)
 
+    @pl.when(moves)
+    def _():
+        pl.semaphore_signal(barrier, inc=1, device_id=host, device_id_type=MESH)
+        pl.semaphore_signal(barrier, inc=1, device_id=home, device_id_type=MESH)
+
     lane = lax.broadcasted_iota(jnp.int32, (COLS, NZ), 1)
     col = lax.broadcasted_iota(jnp.int32, (COLS, NZ), 0) + (ly * BY - HALO)
     col_in = jnp.where((col >= 0) & (col < GY * BY), 1.0, 0.0)
@@ -131,21 +185,7 @@
         at = lx * BX + (i - HALO)
         return jnp.where((at >= 0) & (at < GX * BX), 1.0, 0.0)
 
-    own = slice(HALO, HALO + BY)
-    own_y = pl.ds(OY, BY)
-    wide = pl.ds(Y0, COLS)
-    for r in range(BX):
-        material = material_in[r]
-        base = jnp.zeros((BY, NZ), jnp.float32)
-        for m in range(MATS):
-            base = jnp.where(material == m, table_in[m], base)
-        conductivity = base * jnp.exp(log_in[r])
-        first[1, r, own, :] = conductivity
-        first[1, BX + r, own, :] = head_in[r]
-        first[1, 2 * BX + r, own, :] = source_in[r]
-        second[1, r, own, :] = disp_in[r] * conductivity
-        second[1, BX + r, own, :] = solute_weight_in[r]
-        xe_solute[0, OX + r, own_y, :] = solute_in[r]
+    loads[0].wait()
     kind = boundary_in[...]
     factor = jnp.where(kind == 1, 1.0, jnp.where(kind == 2, 4.0, 0.0)).astype(jnp.float32)
     diagonal_at = lax.broadcasted_iota(jnp.int32, (BY, BY), 0) == lax.broadcasted_iota(
@@ -156,9 +196,59 @@
         spread = jnp.broadcast_to(factor[r : r + 1, :], (BY, BY))
         column = jnp.sum(jnp.where(diagonal_at, spread, 0.0), axis=1, keepdims=True)
         tops = jnp.where(lane[:BY] == r, column, tops)
-    first[1, 3 * BX, own, :] = tops
-
-    pl.semaphore_wait(barrier, len(DIRS) + len(FAR) + 30)
+    tops_home[...] = tops
+    for load in loads[1:4]:
+        load.wait()
+    for r in range(BX):
+        material = material_home[r]
+        base = jnp.zeros((BY, NZ), jnp.float32)
+        for m in range(MATS):
+            base = jnp.where(material == m, table_in[m], base)
+        conductivity = base * jnp.exp(log_in[r])
+        made[0, r] = conductivity
+        made[1, r] = disp_home[r] * conductivity
+
+    class Move:
+        def __init__(self, source, target, sends, recvs, to):
+            self.here = pltpu.make_async_copy(source, target, recvs)
+            self.there = pltpu.make_async_remote_copy(
+                src_ref=source,
+                dst_ref=target,
+                send_sem=sends,
+                recv_sem=recvs,
+                device_id=to,
+                device_id_type=MESH,
+            )
+
+        def start(self):
+            pl.when(stays)(self.here.start)
+            pl.when(moves)(self.there.start)
+
+        def arrive(self):
+            pl.when(stays)(self.here.wait)
+            pl.when(moves)(self.there.wait_recv)
+
+        def wait_send(self):
+            pl.when(moves)(self.there.wait_send)
+
+    moved = []
+    for source, target in (
+        (made.at[0], center(first, 0)),
+        (head_hbm, center(first, 1)),
+        (source_hbm, center(first, 2)),
+        (tops_home, first.at[1, 3 * BX, pl.ds(HALO, BY), :]),
+        (made.at[1], center(second, 0)),
+        (solute_weight_hbm, center(second, 1)),
+        (solute_hbm, xe_solute.at[0, pl.ds(OX, BX), own_y, :]),
+        (head_weight_hbm, head_weight_in),
+        (material_hbm, material_in),
+    ):
+        k = len(moved)
+        moved.append(Move(source, target, move_send.at[k], move_recv.at[k], host))
+
+    pl.semaphore_wait(barrier, len(DIRS) + len(FAR) + 30 + jnp.where(stays, 0, 2))
+    for move in moved[:6]:
+        move.start()
 
     near = lax.broadcasted_iota(jnp.int32, (HALO, NZ), 0)
 
@@ -177,6 +267,7 @@
 
     def exchange(event, source_of, target_of, base, fields, extra=None):
         copies = [launch(event, d, source_of(d), target_of(d)) for d in FACES]
+        parts = []
         for k, (dx, dy) in enumerate(CORNERS):
             at = base
             for radius, read, _ in fields:
@@ -193,8 +284,12 @@
             if extra is not None:
                 corner_out[k, at] = extra[0](dx, dy)
                 at += 1
-            part = pl.ds(base, at - base)
-            copies.append(launch(event, (dx, dy), corner_out.at[k, part], corner_in.at[k, part]))
+            parts.append(pl.ds(base, at - base))
+        copies.extend(
+            launch(event, d, corner_out.at[k, parts[k]], corner_in.at[k, parts[k]])
+            for k, d in enumerate(CORNERS)
+        )
+        started.extend(copies)
 
         def lay():
             for k, (dx, dy) in enumerate(CORNERS):
@@ -210,7 +305,6 @@
                 if extra is not None:
                     extra[1](dx, dy, corner_in[k, at])
 
-        started.extend(copies)
         return copies, lay
 
     def exchange_pack(event, pack, base, radii, extra=None):
@@ -295,7 +389,11 @@
         return copy
 
     started = []
+    for move in moved[:4]:
+        move.arrive()
     got_first = exchange_pack(0, first, 0, (8, 8, 8), 3 * BX)
+    for move in moved[4:6]:
+        move.arrive()
     got_second = exchange_pack(1, second, 13, (9, 8))
     rows = pl.ds(0, BX)
     got_far = [
@@ -305,7 +403,9 @@
         send_to((0, -1), second.at[1, rows, pl.ds(BY, HALO), :], far_y.at[1], 3),
     ]
     started += got_far
-    got_start = exchange_field(2, xe_solute, 22, (0,))
+
+    for move in moved[6:8]:
+        move.start()
 
     at_low, at_high = col == ly * BY - HALO, col == ly * BY + BY + HALO - 1
     low_face = jnp.where(at_low & (col > 0) & (col < GY * BY), 0.5, 0.0)
@@ -331,7 +431,6 @@
             layer = jnp.where(top_lane, 0.0, 0.5 * (row + up(row)))
             czu[field, i] = layer
             under = down(layer)
-            czd[field, i] = under
             if face is not None and face_before is not None:
                 south = pltpu.roll(side, 1, 0)
                 if far:
@@ -355,30 +454,36 @@
             total = face_east * east + face_west * west
             total = total + cy[field, i, here, :] * cur[i, ahead, :]
             total = total + cy[field, i, behind, :] * cur[i, behind, :]
-            total = total + czu[field, i, span, :] * up(mid) + czd[field, i, span, :] * down(mid)
+            layer = czu[field, i, span, :]
+            total = total + layer * up(mid) + down(layer * mid)
             if right is not None:
                 total = total + right[i, span, :]
             nxt[i, here, :] = total * inv[field, i, span, :]
             west, mid, face_west = mid, east, face_east
 
-    def relax(field, even, odd, base, right):
-        def body(t, carry):
-            sweep(field, even.at[t], odd.at[t], 1, ROWS - 1, right)
-            sweep(field, odd.at[t], even.at[t + 1], 2, ROWS - 2, right)
-            return carry
-
-        lax.fori_loop(base, base + 2, body, 0)
-        sweep(field, even.at[base + 2], odd.at[base + 2], 5, ROWS - 5, right)
-        sweep(field, odd.at[base + 2], even.at[base + 3], 6, ROWS - 6, right)
-        sweep(field, even.at[base + 3], odd.at[base + 3], 7, ROWS - 7, right)
-        sweep(field, odd.at[base + 3], even.at[base + 4], OX, OX + BX, right, HALO, BY)
+    def relax(right, base, *chains):
+        def step(t, upward, lo, hi, *y):
+            for field, even, odd in chains:
+                if upward:
+                    sweep(field, even.at[t], odd.at[t], lo, hi, right, *y)
+                else:
+                    sweep(field, odd.at[t], even.at[t + 1], lo, hi, right, *y)
+
+        step(base, True, 1, ROWS - 1)
+        step(base, False, 2, ROWS - 2)
+        step(base + 1, True, 3, ROWS - 3)
+        step(base + 1, False, 4, ROWS - 4)
+        step(base + 2, True, 5, ROWS - 5)
+        step(base + 2, False, 6, ROWS - 6)
+        step(base + 3, True, 7, ROWS - 7)
+        step(base + 3, False, OX, OX + BX, HALO, BY)
 
     def top_of(r):
         tile = first[1, 3 * BX, own, :]
         return jnp.where(lane[:BY] == NZ - 1, pltpu.roll(tile, NZ - 1 - r, 1), 0.0)
 
-    def retrace(field, which):
-        relax(field, lam_even.at[which], lam_odd.at[which], 0, None)
+    def retrace(*pairs):
+        relax(None, 0, *((field, lam_even.at[which], lam_odd.at[which]) for field, which in pairs))
 
     def right_bar(which, r):
         total = lam_even[which, 0, OX + r, own_y, :] + lam_odd[which, 0, OX + r, own_y, :]
@@ -407,13 +512,13 @@
     def gather(field, even, odd, base, which):
         def body(t, carry):
             steps = (
-                ((lam_odd, (which, 3 - t)), (odd, (base + t,)), (even, (base + t,))),
-                ((lam_even, (which, 3 - t)), (even, (base + t + 1,)), (odd, (base + t,))),
+                ((lam_odd, (which, 3 - t)), (even, (base + t,))),
+                ((lam_even, (which, 3 - t)), (odd, (base + t,))),
             )
             for r in range(OX, OX + BX):
                 side = acc_side[field, r - OX]
                 layer = acc_layer[field, r - OX]
-                for (lam, at), _, (old, old_at) in steps:
+                for (lam, at), (old, old_at) in steps:
                     lam_here = lam[(*at, r, own_y)]
                     old_here = old[(*old_at, r, own_y)]
                     side = side + lam_here * around(old, old_at, r)
@@ -421,14 +526,31 @@
                     layer = layer + lam_here * up(old_here) + old_here * up(lam_here)
                 acc_side[field, r - OX] = side
                 acc_layer[field, r - OX] = layer
-            for r in range(OX - 1, OX + BX + 1):
-                drop = acc_drop[field, r - OX + 1, wide, :]
-                for (lam, at), (new, new_at), _ in steps:
-                    drop = drop + lam[(*at, r, wide)] * new[(*new_at, r, wide)]
-                acc_drop[field, r - OX + 1, wide, :] = drop
             return carry
 
         lax.fori_loop(0, 4, body, 0)
+
+    def drops(field, *products):
+        for r in range(OX - 1, OX + BX + 1):
+            drop = acc_drop[field, r - OX + 1, wide, :]
+            for (lam, at), (new, new_at) in products:
+                drop = drop + lam[(*at, r, wide)] * new[(*new_at, r, wide)]
+            acc_drop[field, r - OX + 1, wide, :] = drop
+
+    def last_drop(field, even, base, which):
+        drops(field, ((lam_even, (which, 0)), (even, (base + 4,))))
+
+    def gather_drop(field, even, odd, base, which):
+        def body(t, carry):
+            drops(
+                field,
+                ((lam_odd, (which, 3 - t)), (odd, (base + t,))),
+                ((lam_even, (which, 3 - t)), (even, (base + t + 1,))),
+            )
+            return carry
+
+        lax.fori_loop(0, 3, body, 0)
+        drops(field, ((lam_odd, (which, 0)), (odd, (base + 3,))))
 
     arrive(got_first)
     coefficients(HEAD, lambda i: first[i // BX, i % BX, :, :], False)
@@ -436,8 +558,11 @@
         start = first[i // BX, BX + i % BX, :, :]
         xe_head[0, i, wide, :] = start
         rhs[i] = start + first[i // BX, 2 * BX + i % BX, :, :]
-    relax(HEAD, xe_head, xo_head, 0, rhs)
+    relax(rhs, 0, (HEAD, xe_head, xo_head))
     got_head1 = exchange_field(3, xe_head, 26, (4,))
+    moved[8].start()
+    moved[6].arrive()
+    got_start = exchange_field(2, xe_solute, 22, (0,))
 
     arrive(got_second)
     arrive((got_far, None))
@@ -451,7 +576,8 @@
     coefficients(SOLUTE, spreading, True)
     for i in range(ROWS):
         lam_even[0, 0, i, wide, :] = second[i // BX, BX + i % BX, :, :] * inv[SOLUTE, i]
-    retrace(SOLUTE, 0)
+    retrace((SOLUTE, 0))
+    moved[7].arrive()
     for r in range(BX):
         bar = right_bar(0, r)
         lam_even[1, 0, OX + r, own_y, :] = (head_weight_in[r] + coupling_rate * bar) * inv[
@@ -465,16 +591,15 @@
     arrive(got_head1)
     for i in range(ROWS):
         rhs[i] = xe_head[4, i, wide, :] + first[i // BX, 2 * BX + i % BX, :, :]
-    relax(HEAD, xe_head, xo_head, 4, rhs)
+    relax(rhs, 4, (HEAD, xe_head, xo_head))
     got_head2 = exchange_field(5, xe_head, 38, (8,))
     arrive(got_start)
     for i in range(ROWS):
         rhs[i] = xe_solute[0, i, wide, :] + coupling_rate * xe_head[4, i, wide, :]
-    relax(SOLUTE, xe_solute, xo_solute, 0, rhs)
+    relax(rhs, 0, (SOLUTE, xe_solute, xo_solute))
     got_solute1 = exchange_field(6, xe_solute, 42, (4,))
     arrive(got_lam_mid)
-    retrace(HEAD, 1)
-    retrace(SOLUTE, 2)
+    retrace((HEAD, 1), (SOLUTE, 2))
     for r in range(BX):
         bar = right_bar(1, r) + coupling_rate * right_bar(2, r)
         lam_even[3, 0, OX + r, own_y, :] = (
@@ -482,23 +607,39 @@
         )
     got_lam_h1 = exchange_field(7, lam_even, 46, (3, 0))
 
+    gather(HEAD, xe_head, xo_head, 4, 1)
+    gather_drop(HEAD, xe_head, xo_head, 4, 1)
+    gather(SOLUTE, xe_solute, xo_solute, 0, 2)
+    gather_drop(SOLUTE, xe_solute, xo_solute, 0, 2)
+
     arrive(got_head2)
     arrive(got_solute1)
     for i in range(ROWS):
         rhs[i] = xe_solute[4, i, wide, :] + coupling_rate * xe_head[8, i, wide, :]
-    relax(SOLUTE, xe_solute, xo_solute, 4, rhs)
+    relax(rhs, 4, (SOLUTE, xe_solute, xo_solute))
     got_solute2 = exchange_field(8, xe_solute, None, (8,))
-    gather(HEAD, xe_head, xo_head, 4, 1)
-    gather(SOLUTE, xe_solute, xo_solute, 0, 2)
+    stores = []
+
+    def hand_out(source, k):
+        stores.append(Move(source, fields_out.at[k], store_send.at[k], store_sem.at[k], home))
+        stores[-1].start()
+
+    hand_out(xe_head.at[8, pl.ds(OX, BX), own_y, :], 0)
+    hand_out(xe_solute.at[8, pl.ds(OX, BX), own_y, :], 1)
     arrive(got_lam_h1)
-    retrace(HEAD, 3)
+    retrace((HEAD, 3))
     gather(HEAD, xe_head, xo_head, 0, 3)
-    for r in range(BX):
-        fields_out[0, r] = xe_head[8, OX + r, own_y, :]
-        fields_out[1, r] = xe_solute[8, OX + r, own_y, :]
+    gather_drop(HEAD, xe_head, xo_head, 0, 3)
+    last_drop(HEAD, xe_head, 0, 3)
+    last_drop(HEAD, xe_head, 4, 1)
+    last_drop(SOLUTE, xe_solute, 0, 2)
+    gather(SOLUTE, xe_solute, xo_solute, 4, 0)
+    gather_drop(SOLUTE, xe_solute, xo_solute, 4, 0)
     arrive(got_solute2)
-    gather(SOLUTE, xe_solute, xo_solute, 4, 0)
-
+    last_drop(SOLUTE, xe_solute, 4, 0)
+
+    for move in moved[8:]:
+        move.arrive()
     own_lane = lane[:BY]
     inner_top = own_lane < NZ - 1
     inner_low = own_lane > 0
@@ -524,17 +665,23 @@
     for r in range(BX):
         conductivity = first[1, r, own, :]
         spread_bar = sensitivity(SOLUTE, r)
-        total_bar = sensitivity(HEAD, r) + disp_in[r] * spread_bar
+        dispersivity = second[1, r, own, :] / conductivity
+        total_bar = sensitivity(HEAD, r) + dispersivity * spread_bar
         scaled = total_bar * conductivity
-        fields_out[2, r] = scaled
-        fields_out[3, r] = spread_bar * conductivity
+        grads[0, r] = scaled
+        grads[1, r] = spread_bar * conductivity
         material = material_in[r]
         for m in range(MATS):
             sums[m] = sums[m] + jnp.where(material == m, scaled, 0.0)
+    hand_out(grads.at[0], 2)
+    hand_out(grads.at[1], 3)
     mat_row = lax.broadcasted_iota(jnp.int32, (MATS, NZ), 0)
     partial = jnp.zeros((MATS, NZ), jnp.float32)
     for m in range(MATS):
         partial = jnp.where(mat_row == m, jnp.sum(sums[m], axis=0, keepdims=True), partial)
+    mat_lane = lax.broadcasted_iota(jnp.int32, (MATS, NZ), 1)
+    partial = jnp.sum(partial, axis=1, keepdims=True)
+    partial = jnp.sum(jnp.where(mat_row == mat_lane, partial, 0.0), axis=0, keepdims=True)
 
     def reduce(part, at, device_of, sends, recvs, value):
         part[at] = value
@@ -570,20 +717,23 @@
     started += copies
     copies, partial = reduce(part_b, b_at, b_device, send_b, recv_b, partial)
     started += copies
-    base = jnp.ones((MATS, NZ), jnp.float32)
+    base = jnp.ones((1, NZ), jnp.float32)
     for m in range(MATS):
-        base = jnp.where(mat_row == m, table_in[m], base)
-    summed = jnp.sum(partial, axis=1, keepdims=True)
-    grad_table_out[...] = jnp.broadcast_to(summed, (MATS, NZ)) / base
+        base = jnp.where(lane[:1] == m, table_in[m], base)
+    grad_table_out[...] = partial / base
     for copy in started:
         copy.wait_send()
+    for store in stores:
+        store.arrive()
+    for move in moved + stores:
+        move.wait_send()
 
 
 def hand_over(fields, table, head_out, solute_out, grad_cond_out, grad_disp_out, grad_table_out):
     for k, out in enumerate((head_out, solute_out, grad_cond_out, grad_disp_out)):
         out[...] = fields[k]
     for m in range(MATS):
-        grad_table_out[m] = table[m, 0]
+        grad_table_out[m] = table[0, m]
 
 
 def local(*arrays):
@@ -591,15 +741,30 @@
     block = jax.ShapeDtypeStruct((BX, BY, NZ), f32)
     vmem = pl.BlockSpec(memory_space=pltpu.VMEM)
     smem = pl.BlockSpec(memory_space=pltpu.SMEM)
+    anywhere = pl.BlockSpec(memory_space=pl.ANY)
     fields, table = pl.pallas_call(
         kernel,
         out_shape=(
             jax.ShapeDtypeStruct((4, BX, BY, NZ), f32),
-            jax.ShapeDtypeStruct((MATS, NZ), f32),
+            jax.ShapeDtypeStruct((1, NZ), f32),
         ),
-        in_specs=[smem if k == 6 else vmem for k in range(10)],
-        out_specs=(vmem, vmem),
+        in_specs=[smem if k == 6 else anywhere for k in range(10)],
+        out_specs=(anywhere, vmem),
         scratch_shapes=[
+            pltpu.VMEM((BX, BY, NZ), f32),
+            pltpu.VMEM((BX, BY, NZ), jnp.int32),
+            pltpu.VMEM((BX, BY), jnp.int32),
+            pltpu.VMEM((BX, BY, NZ), f32),
+            pltpu.VMEM((2, BX, BY, NZ), f32),
+            pltpu.VMEM((BX, BY, NZ), jnp.int32),
+            pltpu.VMEM((BX, BY, NZ), f32),
+            pltpu.VMEM((2, BX, BY, NZ), f32),
+            pltpu.VMEM((BY, NZ), f32),
+            pltpu.SemaphoreType.DMA((4,)),
+            pltpu.SemaphoreType.DMA((4,)),
+            pltpu.SemaphoreType.DMA((4,)),
+            pltpu.SemaphoreType.DMA((10,)),
+            pltpu.SemaphoreType.DMA((10,)),
             pltpu.VMEM((3, 3 * BX + 1, COLS, NZ), f32),
             pltpu.VMEM((3, 2 * BX, COLS, NZ), f32),
             pltpu.VMEM((2, BY, NZ), f32),
@@ -608,7 +773,6 @@
             pltpu.VMEM((4, TILES, HALO, NZ), f32),
             pltpu.VMEM((2, ROWS, COLS, NZ), f32),
             pltpu.VMEM((2, ROWS, PAD, NZ), f32),
-            pltpu.VMEM((2, ROWS, COLS, NZ), f32),
             pltpu.VMEM((2, ROWS, COLS, NZ), f32),
             pltpu.VMEM((2, ROWS, COLS, NZ), f32),
             pltpu.VMEM((ROWS, COLS, NZ), f32),
@@ -621,8 +785,8 @@
             pltpu.VMEM((2, BX, BY, NZ), f32),
             pltpu.VMEM((2, BX, BY, NZ), f32),
             pltpu.VMEM((2, BX + 2, PAD, NZ), f32),
-            pltpu.VMEM((16, MATS, NZ), f32),
-            pltpu.VMEM((16, MATS, NZ), f32),
+            pltpu.VMEM((16, 1, NZ), f32),
+            pltpu.VMEM((16, 1, NZ), f32),
             pltpu.SemaphoreType.DMA((9, 8)),
             pltpu.SemaphoreType.DMA((9, 8)),
             pltpu.SemaphoreType.DMA((4,)),

time: 71.5 us -> 67.8 us (0.948)
  Pallas kernels: 70.7 us -> 66.8 us
    pallas_call x1, Pallas kernels: 69 us -> 65.1 us  [local(): pl.pallas_call(kernel, out_shape=(jax.ShapeDtypeStruct((4, BX, BY, NZ), f...]
where the time goes in v2:
time: 67.8 us; the launch traced here: 67.6 us
  Pallas kernels  66.8 us (99%)
  between operations  0.8 us (1%)
    pallas_call x1, Pallas kernels, local(): pl.pallas_call(kernel, out_shape=(jax.ShapeDtypeStruct((4, BX, BY, NZ), f...  65.1 us
    pallas_call x1, Pallas kernels, local(): pl.pallas_call(hand_over, out_shape=(block, block, block, block, jax.Shap...  1.66 us

profile of v2, /device:TPU:1, one launch (start us, length us, event | category | flops | bytes accessed | tf_op | source)
XLA Modules:
  0.0 67.6 jit_solution(6920454634173045725)
XLA Ops:
  0.6 65.1 %window.1 = (f32[4,8,16,128]{3,2,1,0:T(8,128)}, f32[1,128]{1,0:T(1,128)}) custom-call(f32[8,16,128]{2,1,0:T(8,128)} %head_hbm.1, f32[8,16,128]{2,1,0:T(8,128)} %solute_hbm.1, f32[8,16,128]{2,1,0:T(8,128)} %source_hbm.1, f32[8,16,128]{2,1,0:T(8,128)} %log_hbm.1, f32[8,16,128]{2,1,0:T(8,128)} %disp_hbm.1, s32[8,16,128]{2,1,0:T(8,128)} %material_hbm.1, ...), custom_call_target="tpu_custom_call" | custom-call | tf_op jit(solution)/shard_map/window/pallas_call | solution.py:745
  65.7 1.7 %hand_over.1 = (f32[8,16,128]{2,1,0:T(8,128)}, f32[8,16,128]{2,1,0:T(8,128)}, f32[8,16,128]{2,1,0:T(8,128)}, f32[8,16,128]{2,1,0:T(8,128)}, f32[8]{0:T(128)}) custom-call(f32[4,8,16,128]{3,2,1,0:T(8,128)} %get-tuple-element.7.fields, f32[1,128]{1,0:T(1,128)} %get-tuple-element.8.table), custom_call_target="tpu_custom_call" | custom-call | tf_op jit(solution)/shard_map/hand_over/pallas_call | solution.py:804

commit v3 on v2

--- a/solution.py
+++ b/solution.py
@@ -266,7 +266,10 @@
         return copy
 
     def exchange(event, source_of, target_of, base, fields, extra=None):
-        copies = [launch(event, d, source_of(d), target_of(d)) for d in FACES]
+        copies = []
+        late = len(fields) == 1
+        if not late:
+            copies.extend(launch(event, d, source_of(d), target_of(d)) for d in FACES)
         parts = []
         for k, (dx, dy) in enumerate(CORNERS):
             at = base
@@ -289,6 +292,8 @@
             launch(event, d, corner_out.at[k, parts[k]], corner_in.at[k, parts[k]])
             for k, d in enumerate(CORNERS)
         )
+        if late:
+            copies.extend(launch(event, d, source_of(d), target_of(d)) for d in FACES)
         started.extend(copies)
 
         def lay():
@@ -364,7 +369,14 @@
             return HALO, read, write
 
         if base is None:
-            copies = [launch(event, d, source_of(d), target_of(d)) for d in FACES]
+            copies = []
+            for dx, dy in FACES:
+                source, target = source_of((dx, dy)), target_of((dx, dy))
+                if dx != 0:
+                    edge, beyond = (OX + BX - 1, OX - 1) if dx > 0 else (OX, OX + BX)
+                    source = ref.at[(*lead_all, edge, own_y, slice(None))]
+                    target = ref.at[(*lead_all, beyond, own_y, slice(None))]
+                copies.append(launch(event, (dx, dy), source, target))
             started.extend(copies)
             return copies, None
         return exchange(event, source_of, target_of, base, [field(lead) for lead in leads])
@@ -552,6 +564,8 @@
         lax.fori_loop(0, 3, body, 0)
         drops(field, ((lam_odd, (which, 0)), (odd, (base + 3,))))
 
+    moved[6].arrive()
+    got_start = exchange_field(2, xe_solute, 22, (0,))
     arrive(got_first)
     coefficients(HEAD, lambda i: first[i // BX, i % BX, :, :], False)
     for i in range(ROWS):
@@ -560,9 +574,6 @@
         rhs[i] = start + first[i // BX, 2 * BX + i % BX, :, :]
     relax(rhs, 0, (HEAD, xe_head, xo_head))
     got_head1 = exchange_field(3, xe_head, 26, (4,))
-    moved[8].start()
-    moved[6].arrive()
-    got_start = exchange_field(2, xe_solute, 22, (0,))
 
     arrive(got_second)
     arrive((got_far, None))
@@ -587,6 +598,7 @@
             lam_even[0, 4, OX + r, own_y, :] + bar * inv[SOLUTE, OX + r, own, :]
         )
     got_lam_mid = exchange_field(4, lam_even, 30, (1, 0), (2, 0), faces=(pl.ds(1, 2), 0))
+    moved[8].start()
 
     arrive(got_head1)
     for i in range(ROWS):
@@ -713,9 +725,9 @@
             total = total + part[k]
         return copies, total
 
+    copies, partial = reduce(part_b, b_at, b_device, send_b, recv_b, partial)
+    started += copies
     copies, partial = reduce(part_a, a_at, a_device, send_a, recv_a, partial)
-    started += copies
-    copies, partial = reduce(part_b, b_at, b_device, send_b, recv_b, partial)
     started += copies
     base = jnp.ones((1, NZ), jnp.float32)
     for m in range(MATS):

time: 67.8 us -> 65.5 us (0.966)
  Pallas kernels: 66.8 us -> 64.5 us
    pallas_call x1, Pallas kernels: 65.1 us -> 62.8 us  [local(): pl.pallas_call(kernel, out_shape=(jax.ShapeDtypeStruct((4, BX, BY, NZ), f...]
where the time goes in v3:
time: 65.5 us; the launch traced here: 65.3 us
  Pallas kernels  64.5 us (98%)
  between operations  0.8 us (1%)
    pallas_call x1, Pallas kernels, local(): pl.pallas_call(kernel, out_shape=(jax.ShapeDtypeStruct((4, BX, BY, NZ), f...  62.8 us
    pallas_call x1, Pallas kernels, local(): pl.pallas_call(hand_over, out_shape=(block, block, block, block, jax.Shap...  1.66 us

profile of v3, /device:TPU:1, one launch (start us, length us, event | category | flops | bytes accessed | tf_op | source)
XLA Modules:
  0.0 65.3 jit_solution(4782310142340482182)
XLA Ops:
  0.6 62.8 %window.1 = (f32[4,8,16,128]{3,2,1,0:T(8,128)}, f32[1,128]{1,0:T(1,128)}) custom-call(f32[8,16,128]{2,1,0:T(8,128)} %head_hbm.1, f32[8,16,128]{2,1,0:T(8,128)} %solute_hbm.1, f32[8,16,128]{2,1,0:T(8,128)} %source_hbm.1, f32[8,16,128]{2,1,0:T(8,128)} %log_hbm.1, f32[8,16,128]{2,1,0:T(8,128)} %disp_hbm.1, s32[8,16,128]{2,1,0:T(8,128)} %material_hbm.1, ...), custom_call_target="tpu_custom_call" | custom-call | tf_op jit(solution)/shard_map/window/pallas_call | solution.py:757
  63.5 1.7 %hand_over.1 = (f32[8,16,128]{2,1,0:T(8,128)}, f32[8,16,128]{2,1,0:T(8,128)}, f32[8,16,128]{2,1,0:T(8,128)}, f32[8,16,128]{2,1,0:T(8,128)}, f32[8]{0:T(128)}) custom-call(f32[4,8,16,128]{3,2,1,0:T(8,128)} %get-tuple-element.7.fields, f32[1,128]{1,0:T(1,128)} %get-tuple-element.8.table), custom_call_target="tpu_custom_call" | custom-call | tf_op jit(solution)/shard_map/hand_over/pallas_call | solution.py:816

commit v4 on v3

--- a/solution.py
+++ b/solution.py
@@ -636,9 +636,9 @@
         stores.append(Move(source, fields_out.at[k], store_send.at[k], store_sem.at[k], home))
         stores[-1].start()
 
+    arrive(got_lam_h1)
     hand_out(xe_head.at[8, pl.ds(OX, BX), own_y, :], 0)
     hand_out(xe_solute.at[8, pl.ds(OX, BX), own_y, :], 1)
-    arrive(got_lam_h1)
     retrace((HEAD, 3))
     gather(HEAD, xe_head, xo_head, 0, 3)
     gather_drop(HEAD, xe_head, xo_head, 0, 3)
@@ -685,8 +685,6 @@
         material = material_in[r]
         for m in range(MATS):
             sums[m] = sums[m] + jnp.where(material == m, scaled, 0.0)
-    hand_out(grads.at[0], 2)
-    hand_out(grads.at[1], 3)
     mat_row = lax.broadcasted_iota(jnp.int32, (MATS, NZ), 0)
     partial = jnp.zeros((MATS, NZ), jnp.float32)
     for m in range(MATS):
@@ -695,7 +693,7 @@
     partial = jnp.sum(partial, axis=1, keepdims=True)
     partial = jnp.sum(jnp.where(mat_row == mat_lane, partial, 0.0), axis=0, keepdims=True)
 
-    def reduce(part, at, device_of, sends, recvs, value):
+    def reduce(part, at, device_of, sends, recvs, value, meanwhile=None):
         part[at] = value
         copies = []
         for t in range(1, 16):
@@ -710,6 +708,8 @@
                 )
             )
             copies[-1].start()
+        if meanwhile is not None:
+            meanwhile()
         for t in range(1, 16):
             slot = lax.rem(at - t + 16, 16)
             pltpu.make_async_remote_copy(
@@ -725,7 +725,11 @@
             total = total + part[k]
         return copies, total
 
-    copies, partial = reduce(part_b, b_at, b_device, send_b, recv_b, partial)
+    def gradients_home():
+        hand_out(grads.at[0], 2)
+        hand_out(grads.at[1], 3)
+
+    copies, partial = reduce(part_b, b_at, b_device, send_b, recv_b, partial, gradients_home)
     started += copies
     copies, partial = reduce(part_a, a_at, a_device, send_a, recv_a, partial)
     started += copies

time: 65.5 us -> 67.4 us (1.029)
  Pallas kernels: 64.5 us -> 66.3 us
    pallas_call x1, Pallas kernels: 62.8 us -> 64.7 us  [local(): pl.pallas_call(kernel, out_shape=(jax.ShapeDtypeStruct((4, BX, BY, NZ), f...]
where the time goes in v4:
time: 67.4 us; the launch traced here: 67.1 us
  Pallas kernels  66.3 us (98%)
  between operations  0.8 us (1%)
    pallas_call x1, Pallas kernels, local(): pl.pallas_call(kernel, out_shape=(jax.ShapeDtypeStruct((4, BX, BY, NZ), f...  64.7 us
    pallas_call x1, Pallas kernels, local(): pl.pallas_call(hand_over, out_shape=(block, block, block, block, jax.Shap...  1.66 us

profile of v4, /device:TPU:1, one launch (start us, length us, event | category | flops | bytes accessed | tf_op | source)
XLA Modules:
  0.0 67.1 jit_solution(2388982145559044358)
XLA Ops:
  0.6 64.7 %window.1 = (f32[4,8,16,128]{3,2,1,0:T(8,128)}, f32[1,128]{1,0:T(1,128)}) custom-call(f32[8,16,128]{2,1,0:T(8,128)} %head_hbm.1, f32[8,16,128]{2,1,0:T(8,128)} %solute_hbm.1, f32[8,16,128]{2,1,0:T(8,128)} %source_hbm.1, f32[8,16,128]{2,1,0:T(8,128)} %log_hbm.1, f32[8,16,128]{2,1,0:T(8,128)} %disp_hbm.1, s32[8,16,128]{2,1,0:T(8,128)} %material_hbm.1, ...), custom_call_target="tpu_custom_call" | custom-call | tf_op jit(solution)/shard_map/window/pallas_call | solution.py:761
  65.3 1.7 %hand_over.1 = (f32[8,16,128]{2,1,0:T(8,128)}, f32[8,16,128]{2,1,0:T(8,128)}, f32[8,16,128]{2,1,0:T(8,128)}, f32[8,16,128]{2,1,0:T(8,128)}, f32[8]{0:T(128)}) custom-call(f32[4,8,16,128]{3,2,1,0:T(8,128)} %get-tuple-element.7.fields, f32[1,128]{1,0:T(1,128)} %get-tuple-element.8.table), custom_call_target="tpu_custom_call" | custom-call | tf_op jit(solution)/shard_map/hand_over/pallas_call | solution.py:820
